TPU v7x, 128 devices: a whole 4x4x4 slice. The times are simulated.
128 devices in a mesh: dp: 8 (over y, core), expert: 16 (over x, z).
Axes of the slice: x: 4, y: 4, z: 4, core: 2. Of those that a mesh axis runs over, the one named last changes fastest.
Arguments:
- query_rows: bfloat16 [256, 6144], P(('dp', 'expert')), may hold values from -256 to 256
- key_cache: bfloat16 [256, 128, 1024], P(('dp', 'expert')), may hold values from -6 to 6
- value_cache: bfloat16 [256, 128, 1024], P(('dp', 'expert')), may hold values from -6 to 6
- residual: bfloat16 [256, 6144], P(('dp', 'expert')), may hold values from -36 to 36
- norm_gain: float32 [6144], replicated, may hold values from 0.1 to 1.9
- expert_ids: int32 [256, 4], P(('dp', 'expert')), may hold values from 0 to 15, all different within a row; in each aligned block of 32 rows (0 to 31, 32 to 63, ...) at most 16 rows name the same one
- route_weights: float32 [256, 4], P(('dp', 'expert')), may hold values from 0.1 to 0.6
- w_gate: bfloat16 [16, 6144, 5376], P('expert', None, 'dp'), may hold values from -0.078125 to 0.078125
- w_up: bfloat16 [16, 6144, 5376], P('expert', None, 'dp'), may hold values from -0.078125 to 0.078125
- w_down: bfloat16 [16, 5376, 6144], P('expert', 'dp'), may hold values from -0.078125 to 0.078125
Outputs:
- layer_out: bfloat16 [256, 6144], P(('dp', 'expert'))
Inputs may be any that keep to these rules, and one draw needn't show every extreme that they name: `expert_ids`: each row names 4 different experts. In each aligned block of 32 rows (the rows of one index of dp) no expert is named by more than 16 rows, and in some of these blocks one expert is named by exactly 16.
All inputs are finite; a program needn't handle non-finite values.
Results may differ from a plain program's by a relative error of at most 0.006.
Values may be sent and summed in bfloat16 or wider, within the bound.
A program may use at most 128 MiB of HBM per device.

v0:
```python
import jax
import jax.numpy as jnp
from jax import lax
from jax.sharding import PartitionSpec as P

D = 6144
H = 48
KVH = 8
HD = 128


def attend(query_rows, key_cache, value_cache):
    row_count = query_rows.shape[0]
    positions = key_cache.shape[1]
    query_heads = query_rows.reshape(row_count, KVH, H // KVH, HD)
    key_heads = key_cache.reshape(row_count, positions, KVH, HD)
    value_heads = value_cache.reshape(row_count, positions, KVH, HD)
    attn_scores = jnp.einsum(
        "rkgd,rtkd->rkgt", query_heads, key_heads, preferred_element_type=jnp.float32
    ) * HD ** (-0.5)
    row_max = jnp.max(attn_scores, axis=-1, keepdims=True)
    lifted = jnp.exp(attn_scores - row_max)
    attn_probs = (lifted / jnp.sum(lifted, axis=-1, keepdims=True)).astype(jnp.bfloat16)
    attended = jnp.einsum(
        "rkgt,rtkd->rkgd", attn_probs, value_heads, preferred_element_type=jnp.float32
    )
    return attended.reshape(row_count, D)


def layer_norm(hstate, norm_gain):
    widened = hstate.astype(jnp.float32)
    row_mean = jnp.mean(widened, axis=-1, keepdims=True)
    centered = widened - row_mean
    row_var = jnp.mean(centered * centered, axis=-1, keepdims=True)
    return (centered * lax.rsqrt(row_var + 1e-05) * norm_gain).astype(jnp.bfloat16)


def body(
    query_rows,
    key_cache,
    value_cache,
    residual,
    norm_gain,
    expert_ids,
    route_weights,
    w_gate,
    w_up,
    w_down,
):
    experts = lax.axis_size("expert")
    dp_count = lax.axis_size("dp")
    row_count = query_rows.shape[0]
    gate_local = w_gate[0]
    up_local = w_up[0]
    down_local = w_down[0]
    attended = attend(query_rows, key_cache, value_cache)
    hstate = (residual.astype(jnp.float32) + attended).astype(jnp.bfloat16)
    normed = layer_norm(hstate, norm_gain)
    chosen = expert_ids[:, :, None] == jnp.arange(experts, dtype=jnp.int32)[None, None, :]
    picked = jnp.any(chosen, axis=1)
    weight_table = jnp.sum(jnp.where(chosen, route_weights[:, :, None], 0.0), axis=1)
    picked_t = jnp.transpose(picked)
    outgoing = jnp.where(picked_t[:, :, None], normed[None, :, :], jnp.zeros((), jnp.bfloat16))
    copies = jnp.broadcast_to(outgoing[None], (dp_count, experts, row_count, D)).reshape(
        dp_count * experts, row_count, D
    )
    item_block = lax.all_to_all(copies, ("dp", "expert"), split_axis=0, concat_axis=0, tiled=True)
    row_total = item_block.shape[1]
    slot_rows = item_block.reshape(-1, D)
    gate_proj = jnp.dot(slot_rows, gate_local, preferred_element_type=jnp.float32)
    up_proj = jnp.dot(slot_rows, up_local, preferred_element_type=jnp.float32)
    activated = (jax.nn.silu(gate_proj) * up_proj).astype(jnp.bfloat16)
    partial_value = jnp.dot(activated, down_local, preferred_element_type=jnp.float32).astype(
        jnp.bfloat16
    )
    partials = partial_value.reshape(item_block.shape[0], row_total, D)
    arrived_back = lax.all_to_all(
        partials, ("dp", "expert"), split_axis=0, concat_axis=0, tiled=True
    )
    summed = jnp.sum(
        arrived_back.reshape(dp_count, experts, row_count, D).astype(jnp.float32), axis=0
    )
    returned = summed.astype(jnp.bfloat16)
    mixed = jnp.einsum("re,erd->rd", weight_table, returned.astype(jnp.float32))
    return (hstate.astype(jnp.float32) + mixed).astype(jnp.bfloat16)


def solution(mesh):
    return jax.shard_map(
        body,
        mesh=mesh,
        in_specs=(
            P(("dp", "expert"), None),
            P(("dp", "expert"), None, None),
            P(("dp", "expert"), None, None),
            P(("dp", "expert"), None),
            P(),
            P(("dp", "expert"), None),
            P(("dp", "expert"), None),
            P("expert", None, "dp"),
            P("expert", None, "dp"),
            P("expert", "dp", None),
        ),
        out_specs=P(("dp", "expert"), None),
        check_vma=False,
    )
```

profile of v0, /device:TPU:0, one launch (start us, length us, event | category | flops | bytes accessed | tf_op | source)
XLA Modules:
  0.0 150.8 jit_solution(5465142897954274579)
XLA Ops:
  0.0 0.0 copy-start
  0.0 0.8 reshape.45
  0.8 0.2 copy-done
  1.1 0.4 convolution_multiply_fusion
  1.4 0.2 fusion.39
  1.6 1.3 fusion.22
  3.0 0.9 convert_reduce_fusion
  3.9 0.2 fusion.32
  4.2 0.8 fusion.37
  5.0 0.1 copy.19
  5.1 0.8 fusion.34
  5.9 0.3 broadcast_select_fusion
  6.2 2.1 %broadcast_in_dim.53 = bf16[8,16,2,6144]{3,2,1,0:T(2,128)(2,1)S(1)} broadcast(bf16[16,2,6144]{2,1,0:T(2,128)(2,1)S(1)} %broadcast_select_fusion), dimensions={1,2,3} | broadcast | bytes 3538944 | tf_op jit(solution)/shard_map/broadcast_in_dim | solution.py:64
  8.4 51.7 %all_to_all.10 = bf16[128,2,6144]{2,1,0:T(2,128)(2,1)} all-to-all(bf16[128,2,6144]{2,1,0:T(2,128)(2,1)S(1)} %bitcast.45), channel_id=1, replica_groups=mesh['dp'=8,'expert'=16] {'dp','expert'}, dimensions={0} | all-to-all | bytes 6291456 | tf_op jit(solution)/shard_map/all_to_all | solution.py:67
  60.1 7.3 %reshape.50 = bf16[256,6144]{1,0:T(8,128)(2,1)} reshape(bf16[128,2,6144]{2,1,0:T(2,128)(2,1)} %all_to_all.10) | data formatting | bytes 6291456 | tf_op jit(solution)/shard_map/reshape | solution.py:69
  67.4 6.6 %fusion.5 = f32[256,672]{0,1:T(8,128)S(1)} fusion(bf16[256,6144]{1,0:T(8,128)(2,1)} %reshape.50, bf16[1,6144,672]{1,2,0:T(8,128)(2,1)} %param.17), kind=kOutput, calls=%fused_computation.5 | convolution fusion | flops 2113929216 | bytes 12091392 | tf_op jit(solution)/shard_map/dot_general | solution.py:70
  74.0 17.4 %fusion.7 = bf16[256,6144]{1,0:T(8,128)(2,1)} fusion(bf16[1,672,6144]{2,1,0:T(8,128)(2,1)} %param.19, bf16[256,6144]{1,0:T(8,128)(2,1)} %reshape.50, bf16[1,6144,672]{1,2,0:T(8,128)(2,1)} %param.18, f32[256,672]{0,1:T(8,128)S(1)} %fusion.5), kind=kOutput, calls=%fused_computation.7 | convolution fusion | flops 4230463488 | bytes 23494656 | tf_op jit(solution)/shard_map/dot_general | solution.py:73
  91.5 0.0 copy-start.1
  91.5 0.0 copy-start.2
  91.5 7.1 %reshape.51 = bf16[128,2,6144]{2,1,0:T(2,128)(2,1)} reshape(bf16[256,6144]{1,0:T(8,128)(2,1)} %fusion.7) | data formatting | bytes 6291456 | tf_op jit(solution)/shard_map/reshape | solution.py:76
  98.6 6.0 %all-to-all-start.1 = ((bf16[128,2,6144]{2,1,0:T(2,128)(2,1)}), bf16[128,2,6144]{2,1,0:T(2,128)(2,1)}, u32[]{:S(2)}, u32[]{:S(2)}) async-start(bf16[128,2,6144]{2,1,0:T(2,128)(2,1)} %reshape.51), calls=%async_computation.1 | async-start | bytes 6291456 | tf_op jit(solution)/shard_map/all_to_all | solution.py:77
  104.5 0.0 copy-done.1
  104.5 0.0 copy-done.2
  104.5 0.1 select_reduce_fusion
  104.6 40.2 %all-to-all-done.1 = bf16[128,2,6144]{2,1,0:T(2,128)(2,1)} async-done(((bf16[128,2,6144]{2,1,0:T(2,128)(2,1)}), bf16[128,2,6144]{2,1,0:T(2,128)(2,1)}, u32[]{:S(2)}, u32[]{:S(2)}) %all-to-all-start.1) | async-done | bytes 3145760 | tf_op jit(solution)/shard_map/all_to_all | solution.py:77
  144.8 5.0 %reduce_sum.52 = bf16[16,2,6144]{2,1,0:T(2,128)(2,1)S(1)} reduce(bf16[8,16,2,6144]{3,2,1,0:T(2,128)(2,1)} %bitcast.7, bf16[]{:T(256)} %constant.18.clone.1), dimensions={0}, to_apply=%region_6.7 | reduce | flops 1376256 | bytes 3538946 | tf_op jit(solution)/shard_map/reduce_sum | solution.py:80
  149.8 0.3 fusion.27
  150.1 0.6 fusion.35
  (3 shorter events, 0.1 us)
Async XLA Ops:
  0.0 1.1 copy-start
  91.5 13.0 %copy-start.1 = (f32[2,4]{1,0:T(2,128)S(1)}, f32[2,4]{1,0:T(2,128)}, u32[]{:S(2)}) copy-start(f32[2,4]{1,0:T(2,128)} %param.16) | copy-start | bytes 100
  91.5 13.1 %copy-start.2 = (s32[2,4]{1,0:T(2,128)S(1)}, s32[2,4]{1,0:T(2,128)}, u32[]{:S(2)}) copy-start(s32[2,4]{1,0:T(2,128)} %param.15) | copy-start | bytes 100
  98.6 46.3 %all-to-all-start.1 = ((bf16[128,2,6144]{2,1,0:T(2,128)(2,1)}), bf16[128,2,6144]{2,1,0:T(2,128)(2,1)}, u32[]{:S(2)}, u32[]{:S(2)}) async-start(bf16[128,2,6144]{2,1,0:T(2,128)(2,1)} %reshape.51), calls=%async_computation.1 | async-start | bytes 6291456 | tf_op jit(solution)/shard_map/all_to_all | solution.py:77
where the time goes:
time: 152 us; the launch traced here: 151 us
  blocking collectives  51.7 us (34%)
  waiting for transfers between devices  40.2 us (26%)
  matrix products  26.1 us (17%)
  local copies, waits for them, and re-layouts  17.7 us (12%)
  other arithmetic  9.02 us (6%)
  starting transfers between devices  5.95 us (4%)
    all_to_all x1, blocking collectives, body(): lax.all_to_all(copies, ('dp', 'expert'), split_axis=0, concat_axis=0, til...  51.7 us
    all_to_all x1, waiting for transfers between devices, body(): lax.all_to_all(partials, ('dp', 'expert'), split_axis=0, concat_axis=0, t...  40.2 us
    dot_general x1, matrix products, body(): jnp.dot(activated, down_local, preferred_element_type=jnp.float32)  17.4 us
    reshape x1, local copies, waits for them, and re-layouts, body(): slot_rows = item_block.reshape(-1, D)  7.32 us
    reshape x1, local copies, waits for them, and re-layouts, body(): partials = partial_value.reshape(item_block.shape[0], row_total, D)  7.08 us
    dot_general x1, matrix products, body(): jnp.dot(slot_rows, gate_local, preferred_element_type=jnp.float32)  6.63 us
    all_to_all x1, starting transfers between devices, body(): lax.all_to_all(partials, ('dp', 'expert'), split_axis=0, concat_axis=0, t...  5.95 us
    reduce_sum x1, other arithmetic, body(): jnp.sum(arrived_back.reshape(dp_count, experts, row_count, D).astype(jnp....  4.99 us
  transfers between devices with their start and end apart: 1, of which 1 were waited for; matrix products, arithmetic and copies ran while one was open for 0% of the time, Pallas kernels for 0%

commit v1 on v0

v1 whole, which is shorter than its diff:
```python
import jax
import jax.numpy as jnp
from jax import lax
from jax.experimental import pallas as pl
from jax.experimental.pallas import tpu as pltpu
from jax.sharding import PartitionSpec as P

MESH = pl.DeviceIdType.MESH
D = 6144
H = 48
KVH = 8
HD = 128
PER = H // KVH
TOPK = 4
CTX = 128
NY, NX, NZ = 4, 4, 4
PLANE = NX * NZ
CAP = 16
FF = 672
NC = 3
HC = H // NC
CW = D // NC
BF = jnp.bfloat16
F32 = jnp.float32


def bytes_wait(ref, sem):
    pltpu.make_async_copy(ref, ref, sem).wait()


def across(a, b):
    return lax.dot_general(a, b, (((1,), (1,)), ((), ())), preferred_element_type=F32)


def kernel(
    ids_s,
    wts_s,
    q_ref,
    res_ref,
    gain_ref,
    key_hbm,
    val_hbm,
    gate_hbm,
    up_hbm,
    down_hbm,
    out_ref,
    key_v,
    val_v,
    gate_v,
    up_v,
    down_v,
    rows_q,
    rows_res,
    hst,
    mine,
    mine_ids,
    ids_in,
    x_in,
    flat,
    x_t,
    x_all,
    acc_g,
    acc_u,
    act,
    part,
    pair_in,
    summed,
    y_in,
    ret,
    r_in,
    sem_kv,
    sem_w,
    send_i,
    recv_i,
    send_a,
    recv_a,
    send_y,
    recv_y,
    send_p,
    recv_p,
    send_q,
    recv_q,
    send_z,
    recv_z,
    send_r,
    recv_r,
):
    p = lax.axis_index("dp")
    e = lax.axis_index("expert")
    y, core = p // 2, lax.rem(p, 2)
    x, z = e // NZ, lax.rem(e, NZ)
    offsets = [(i, j) for i in range(NX) for j in range(NZ)]

    def plane_dev(i, j):
        return (p, lax.rem(x + i + NX, NX) * NZ + lax.rem(z + j + NZ, NZ))

    def y_dev(dy):
        return (lax.rem(y + dy + NY, NY) * 2 + core, e)

    pair = (y * 2 + 1 - core, e)

    loads = []
    for r in range(2):
        for n, (src, dst) in enumerate(((key_hbm, key_v), (val_hbm, val_v))):
            cp = pltpu.make_async_copy(src.at[r], dst.at[r], sem_kv.at[2 * r + n])
            cp.start()
            loads.append(cp)
    w_loads = []
    for n, (src, dst) in enumerate(((gate_hbm, gate_v), (up_hbm, up_v), (down_hbm, down_v))):
        cp = pltpu.make_async_copy(src.at[0], dst, sem_w.at[n])
        cp.start()
        w_loads.append(cp)

    barrier = pltpu.get_barrier_semaphore()
    greet = [plane_dev(i, j) for i, j in offsets[1:]] + [y_dev(d) for d in range(1, NY)] + [pair]
    for dev in greet:
        pl.semaphore_signal(barrier, inc=1, device_id=dev, device_id_type=MESH)

    sub = lax.broadcasted_iota(jnp.int32, (8, 128), 0)
    lane = lax.broadcasted_iota(jnp.int32, (8, 128), 1)
    tile = jnp.zeros((8, 128), F32)
    for r in range(2):
        for k in range(TOPK):
            tile = jnp.where((sub == r) & (lane == ids_s[r, k]), 1.0, tile)
    mine_ids[...] = tile

    qf = q_ref[...].astype(F32)
    rf = res_ref[...].astype(F32)
    for h in range(H):
        rows_q[pl.ds(h, 2, stride=H), :] = qf[:, h * HD : (h + 1) * HD]
        rows_res[pl.ds(h, 2, stride=H), :] = rf[:, h * HD : (h + 1) * HD]
    head = lax.broadcasted_iota(jnp.int32, (H, HD), 0)
    masks = [(head >= PER * g) & (head < PER * (g + 1)) for g in range(KVH)]
    gain = gain_ref[...]
    for r in range(2):
        q = rows_q[pl.ds(r * H, H), :]
        q_wide = jnp.concatenate([jnp.where(m, q, 0.0) for m in masks], axis=1).astype(BF)
        loads[2 * r].wait()
        scores = lax.dot_general(
            q_wide, key_v[r], (((1,), (1,)), ((), ())), preferred_element_type=F32
        ) * HD ** (-0.5)
        lifted = jnp.exp(scores - jnp.max(scores, axis=1, keepdims=True))
        probs = (lifted / jnp.sum(lifted, axis=1, keepdims=True)).astype(BF)
        loads[2 * r + 1].wait()
        wide = jnp.dot(probs, val_v[r], preferred_element_type=F32)
        attended = jnp.zeros((H, HD), F32)
        for g in range(KVH):
            attended = jnp.where(masks[g], wide[:, g * HD : (g + 1) * HD], attended)
        hstate = (rows_res[pl.ds(r * H, H), :] + attended).astype(BF).astype(F32)
        hst[r] = hstate
        mean = jnp.sum(hstate) * (1.0 / D)
        centered = hstate - mean
        var = jnp.sum(centered * centered) * (1.0 / D)
        normed = (centered * lax.rsqrt(var + 1e-05) * gain).astype(BF)
        mine[r] = normed
        x_in[0, r] = normed

    pl.semaphore_wait(barrier, len(greet))

    for n, (i, j) in enumerate(offsets):
        if n:
            pltpu.make_async_remote_copy(
                src_ref=mine_ids, dst_ref=ids_in.at[n], send_sem=send_i.at[0],
                recv_sem=recv_i.at[0], device_id=plane_dev(i, j), device_id_type=MESH,
            ).start()
    for c in range(NC):
        for n, (i, j) in enumerate(offsets):
            if n:
                pltpu.make_async_remote_copy(
                    src_ref=mine.at[:, pl.ds(c * HC, HC)],
                    dst_ref=x_in.at[n, :, pl.ds(c * HC, HC)],
                    send_sem=send_a.at[c], recv_sem=recv_a.at[c],
                    device_id=plane_dev(i, j), device_id_type=MESH,
                ).start()
    ids_in[0] = mine_ids[...]
    bytes_wait(ids_in.at[pl.ds(1, PLANE - 1)], recv_i.at[0])

    table = ids_in[...].reshape(PLANE * 8, 128)
    rowi = lax.broadcasted_iota(jnp.int32, (2 * PLANE, PLANE * 8), 0)
    coli = lax.broadcasted_iota(jnp.int32, (2 * PLANE, PLANE * 8), 1)
    squeeze = jnp.where(coli == 4 * rowi - 3 * (rowi & 1), 1.0, 0.0)
    named = jnp.dot(squeeze, table, preferred_element_type=F32)
    mine_lane = lax.broadcasted_iota(jnp.int32, (2 * PLANE, 128), 1)
    picked_c = jnp.sum(jnp.where(mine_lane == e, named, 0.0), axis=1, keepdims=True)
    picked_b = jnp.broadcast_to(picked_c, (2 * PLANE, 128))
    ri = lax.broadcasted_iota(jnp.int32, (2 * PLANE, 2 * PLANE), 0)
    ci = lax.broadcasted_iota(jnp.int32, (2 * PLANE, 2 * PLANE), 1)
    below = jnp.where(ci < ri, 1.0, 0.0)
    rank_b = jnp.dot(below, picked_b, preferred_element_type=F32)
    spread_f = jnp.where(
        (rank_b == mine_lane.astype(F32)) & (picked_b > 0.5), 1.0, 0.0
    )
    spread = spread_f[:, :CAP].astype(BF)
    ident = jnp.where(ri == ci, 1.0, 0.0)
    pick = lax.dot_general(
        spread_f, ident, (((0,), (0,)), ((), ())), preferred_element_type=F32
    )[:CAP, :].astype(BF)

    def forward(c, dy):
        cp = pltpu.make_async_remote_copy(
            src_ref=x_all.at[c, dy], dst_ref=x_all.at[c, NY + dy], send_sem=send_p.at[c, dy],
            recv_sem=recv_p.at[c, dy], device_id=pair, device_id_type=MESH,
        )
        cp.start()
        return cp

    pair_copies = []
    for c in range(NC):
        bytes_wait(x_in.at[pl.ds(1, PLANE - 1), :, pl.ds(c * HC, HC)], recv_a.at[c])
        flat[...] = (
            x_in[:, :, c * HC : (c + 1) * HC, :].astype(F32).reshape(2 * PLANE * HC, HD)
        )
        for s in range(HC):
            x_t[:, s * HD : (s + 1) * HD] = flat[pl.ds(s, 2 * PLANE, stride=HC), :].astype(BF)
        x_all[c, 0] = jnp.dot(pick, x_t[...], preferred_element_type=F32).astype(BF)
        for dy in range(1, NY):
            pltpu.make_async_remote_copy(
                src_ref=x_all.at[c, 0], dst_ref=x_all.at[c, dy], send_sem=send_y.at[c],
                recv_sem=recv_y.at[c, dy], device_id=y_dev(dy), device_id_type=MESH,
            ).start()
        pair_copies.append(forward(c, 0))

    for c in range(NC):
        for dy in range(1, NY):
            bytes_wait(x_all.at[c, dy], recv_y.at[c, dy])
            pair_copies.append(forward(c, dy))
        for dy in range(NY):
            bytes_wait(x_all.at[c, NY + dy], recv_p.at[c, dy])
        if c == 0:
            w_loads[0].wait()
            w_loads[1].wait()
        block = x_all[c].reshape(2 * NY * CAP, CW)
        gate = across(gate_v[:, c * CW : (c + 1) * CW], block)
        up = across(up_v[:, c * CW : (c + 1) * CW], block)
        if c < NC - 1:
            acc_g[...] = gate if c == 0 else acc_g[...] + gate
            acc_u[...] = up if c == 0 else acc_u[...] + up
        else:
            gate = acc_g[...] + gate
            up = acc_u[...] + up
            act[...] = jnp.transpose(gate / (1.0 + jnp.exp(-gate)) * up).astype(BF)

    w_loads[2].wait()

    def down(n):
        out = jnp.dot(
            act[...], down_v[:, n * CW : (n + 1) * CW], preferred_element_type=F32
        ).astype(BF)
        part[n] = out.reshape(2 * NY, CAP, CW)
        pltpu.make_async_remote_copy(
            src_ref=part.at[n, pl.ds(NY, NY)], dst_ref=pair_in.at[n], send_sem=send_q.at[n],
            recv_sem=recv_q.at[n], device_id=pair, device_id_type=MESH,
        ).start()

    def pair_sum(n):
        bytes_wait(pair_in.at[n], recv_q.at[n])
        summed[n] = (part[n, :NY].astype(F32) + pair_in[n].astype(F32)).astype(BF)
        for dy in range(1, NY):
            pltpu.make_async_remote_copy(
                src_ref=summed.at[n, dy], dst_ref=y_in.at[n, dy - 1], send_sem=send_z.at[n],
                recv_sem=recv_z.at[n], device_id=y_dev(-dy), device_id_type=MESH,
            ).start()

    for n in range(NC):
        down(n)
        if n:
            pair_sum(n - 1)
    pair_sum(NC - 1)

    for n in range(NC):
        bytes_wait(y_in.at[n], recv_z.at[n])
        total = summed[n, 0].astype(F32)
        for dy in range(NY - 1):
            total = total + y_in[n, dy].astype(F32)
        back = jnp.dot(spread, total.astype(BF), preferred_element_type=F32)
        for s in range(HC):
            flat[pl.ds(s, 2 * PLANE, stride=HC), :] = back[:, s * HD : (s + 1) * HD]
        ret[n] = flat[...].astype(BF).reshape(PLANE, 2, HC, HD)
        for m, (i, j) in enumerate(offsets):
            if m:
                pltpu.make_async_remote_copy(
                    src_ref=ret.at[n, m], dst_ref=r_in.at[n, m], send_sem=send_r.at[n],
                    recv_sem=recv_r.at[n], device_id=plane_dev(-i, -j), device_id_type=MESH,
                ).start()

    weights = []
    for r in range(2):
        row = []
        for i, j in offsets:
            expert = plane_dev(i, j)[1]
            w = jnp.float32(0.0)
            for k in range(TOPK):
                w = w + jnp.where(ids_s[r, k] == expert, wts_s[r, k], 0.0)
            row.append(w)
        weights.append(row)
    for n in range(NC):
        bytes_wait(r_in.at[n, pl.ds(1, PLANE - 1)], recv_r.at[n])
        for r in range(2):
            total = hst[r, n * HC : (n + 1) * HC, :]
            for m in range(PLANE):
                got = ret[n, 0, r] if m == 0 else r_in[n, m, r]
                total = total + weights[r][m] * got.astype(F32)
            out_ref[r, n * HC : (n + 1) * HC, :] = total.astype(BF)

    bytes_wait(ids_in.at[pl.ds(1, PLANE - 1)], send_i.at[0])
    for c in range(NC):
        bytes_wait(x_in.at[pl.ds(1, PLANE - 1), :, pl.ds(c * HC, HC)], send_a.at[c])
        bytes_wait(x_all.at[c, pl.ds(1, NY - 1)], send_y.at[c])
        bytes_wait(pair_in.at[c], send_q.at[c])
        bytes_wait(y_in.at[c], send_z.at[c])
        bytes_wait(r_in.at[c, pl.ds(1, PLANE - 1)], send_r.at[c])
    for cp in pair_copies:
        cp.wait_send()


def body(q, key_cache, value_cache, residual, norm_gain, ids, wts, w_gate, w_up, w_down):
    vmem = pl.BlockSpec(memory_space=pltpu.VMEM)
    smem = pl.BlockSpec(memory_space=pltpu.SMEM)
    hbm = pl.BlockSpec(memory_space=pl.ANY)
    dma = pltpu.SemaphoreType.DMA
    out = pl.pallas_call(
        kernel,
        out_shape=jax.ShapeDtypeStruct((2, H, HD), BF),
        in_specs=[smem, smem, vmem, vmem, vmem] + [hbm] * 5,
        out_specs=vmem,
        scratch_shapes=[
            pltpu.VMEM((2, CTX, KVH * HD), BF),
            pltpu.VMEM((2, CTX, KVH * HD), BF),
            pltpu.VMEM((FF, D), BF),
            pltpu.VMEM((FF, D), BF),
            pltpu.VMEM((FF, D), BF),
            pltpu.VMEM((2 * H, HD), F32),
            pltpu.VMEM((2 * H, HD), F32),
            pltpu.VMEM((2, H, HD), F32),
            pltpu.VMEM((2, H, HD), BF),
            pltpu.VMEM((8, 128), F32),
            pltpu.VMEM((PLANE, 8, 128), F32),
            pltpu.VMEM((PLANE, 2, H, HD), BF),
            pltpu.VMEM((2 * PLANE * HC, HD), F32),
            pltpu.VMEM((2 * PLANE, CW), BF),
            pltpu.VMEM((NC, 2 * NY, CAP, CW), BF),
            pltpu.VMEM((FF, 2 * NY * CAP), F32),
            pltpu.VMEM((FF, 2 * NY * CAP), F32),
            pltpu.VMEM((2 * NY * CAP, FF), BF),
            pltpu.VMEM((NC, 2 * NY, CAP, CW), BF),
            pltpu.VMEM((NC, NY, CAP, CW), BF),
            pltpu.VMEM((NC, NY, CAP, CW), BF),
            pltpu.VMEM((NC, NY - 1, CAP, CW), BF),
            pltpu.VMEM((NC, PLANE, 2, HC, HD), BF),
            pltpu.VMEM((NC, PLANE, 2, HC, HD), BF),
            dma((4,)),
            dma((3,)),
            dma((1,)),
            dma((1,)),
            dma((NC,)),
            dma((NC,)),
            dma((NC,)),
            dma((NC, NY)),
            dma((NC, NY)),
            dma((NC, NY)),
            dma((NC,)),
            dma((NC,)),
            dma((NC,)),
            dma((NC,)),
            dma((NC,)),
            dma((NC,)),
        ],
        compiler_params=pltpu.CompilerParams(
            collective_id=0, has_side_effects=True, vmem_limit_bytes=56 * 1024 * 1024
        ),
        cost_estimate=pl.CostEstimate(
            flops=6 * 128 * D * FF, bytes_accessed=3 * 2 * D * FF, transcendentals=128 * FF
        ),
        name="decode_layer",
    )(
        ids,
        wts,
        q,
        residual,
        norm_gain.reshape(H, HD),
        key_cache,
        value_cache,
        jnp.swapaxes(w_gate, 1, 2),
        jnp.swapaxes(w_up, 1, 2),
        w_down,
    )
    return out.reshape(2, D)


def solution(mesh):
    return jax.shard_map(
        body,
        mesh=mesh,
        in_specs=(
            P(("dp", "expert"), None),
            P(("dp", "expert"), None, None),
            P(("dp", "expert"), None, None),
            P(("dp", "expert"), None),
            P(),
            P(("dp", "expert"), None),
            P(("dp", "expert"), None),
            P("expert", None, "dp"),
            P("expert", None, "dp"),
            P("expert", "dp", None),
        ),
        out_specs=P(("dp", "expert"), None),
        check_vma=False,
    )
```

time: 152 us -> 51.9 us (0.34)
  blocking collectives: 51.7 us -> 0 us
  Pallas kernels: 0 us -> 50.3 us
  waiting for transfers between devices: 40.2 us -> 0 us
  matrix products: 26.1 us -> 0 us
  local copies, waits for them, and re-layouts: 17.7 us -> 1.36 us
  other arithmetic: 9.02 us -> 0 us
  starting transfers between devices: 5.95 us -> 0 us
    all_to_all x1 -> x0, blocking collectives: 51.7 us -> none  [body(): lax.all_to_all(copies, ('dp', 'expert'), split_axis=0, concat_axis=0, til...]
    pallas_call x0 -> x1, Pallas kernels: none -> 50.3 us  [body(): pl.pallas_call(kernel, out_shape=jax.ShapeDtypeStruct((2, H, HD), BF), in...]
    all_to_all x1 -> x0, waiting for transfers between devices: 40.2 us -> none  [body(): lax.all_to_all(partials, ('dp', 'expert'), split_axis=0, concat_axis=0, t...]
    dot_general x5 -> x0, matrix products: 26.1 us -> none  [the longest x1 17.4 us: body(): jnp.dot(activated, down_local, preferred_element_type=jnp.float32)]
    reshape x4 -> x0, local copies, waits for them, and re-layouts: 15.3 us -> none  [the longest x1 7.32 us: body(): slot_rows = item_block.reshape(-1, D)]
    reduce_sum x4 -> x0, other arithmetic: 6.22 us -> none  [the longest x1 4.99 us: body(): jnp.sum(arrived_back.reshape(dp_count, experts, row_count, D).astype(jnp....]
    all_to_all x1 -> x0, starting transfers between devices: 5.95 us -> none  [body(): lax.all_to_all(partials, ('dp', 'expert'), split_axis=0, concat_axis=0, t...]
    broadcast_in_dim x1 -> x0, local copies, waits for them, and re-layouts: 2.12 us -> none  [body(): jnp.broadcast_to(outgoing[None], (dp_count, experts, row_count, D))]
  transfers between devices with their start and end apart: 1 -> 0, of which waited for: 1 -> 0; matrix products, arithmetic and copies ran while one was open for 0% -> 0% of each run, Pallas kernels for 0% -> 0%
where the time goes in v1:
time: 51.9 us; the launch traced here: 51.7 us
  Pallas kernels  50.3 us (97%)
  local copies, waits for them, and re-layouts  1.36 us (3%)
    pallas_call x1, Pallas kernels, body(): pl.pallas_call(kernel, out_shape=jax.ShapeDtypeStruct((2, H, HD), BF), in...  50.3 us
    unnamed x1, local copies, waits for them, and re-layouts  1.36 us

profile of v1, /device:TPU:0, one launch (start us, length us, event | category | flops | bytes accessed | tf_op | source)
XLA Modules:
  0.0 51.7 jit_solution(11945963932238457665)
XLA Ops:
  0.0 50.3 %decode_layer.1 = bf16[2,48,128]{2,1,0:T(8,128)(2,1)} custom-call(s32[2,4]{1,0:T(2,128)} %ids_s.1, f32[2,4]{1,0:T(2,128)} %wts_s.1, bf16[2,6144]{1,0:T(2,128)(2,1)} %q_ref.1, bf16[2,6144]{1,0:T(2,128)(2,1)} %res_ref.1, f32[48,128]{1,0:T(8,128)} %bitcast.10, bf16[2,128,1024]{2,1,0:T(8,128)(2,1)} %key_hbm.1, bf16[2,128,1024]{2,1,0:T(8,128)(2,1)} %val_hbm.1, ...), custom_call_target="tpu_custom_call" | custom-call | flops 3170893824 | bytes 24772608 | tf_op jit(solution)/shard_map/decode_layer/pallas_call | solution.py:321
  50.3 1.4 %copy.13 = bf16[1,2,48,128]{3,1,2,0:T(2,128)(2,1)} copy(bf16[1,2,48,128]{3,2,1,0:T(8,128)(2,1)} %bitcast.9) | data formatting | bytes 49152

commit v2 on v1

--- a/solution.py
+++ b/solution.py
@@ -17,7 +17,10 @@
 PLANE = NX * NZ
 CAP = 16
 FF = 672
-NC = 3
+NC = 6
+LAG = 3
+EARLY = 4
+FIRST = 4
 HC = H // NC
 CW = D // NC
 BF = jnp.bfloat16
@@ -32,23 +35,34 @@
     return lax.dot_general(a, b, (((1,), (1,)), ((), ())), preferred_element_type=F32)
 
 
+def total_of(a):
+    return jnp.sum(jnp.sum(a, axis=0, keepdims=True), axis=1, keepdims=True)
+
+
 def kernel(
-    ids_s,
-    wts_s,
-    q_ref,
-    res_ref,
-    gain_ref,
+    ids_hbm,
+    wts_hbm,
+    q_hbm,
+    res_hbm,
+    gain_hbm,
     key_hbm,
     val_hbm,
     gate_hbm,
     up_hbm,
     down_hbm,
     out_ref,
+    ids_s,
+    wts_s,
+    q_ref,
+    res_ref,
+    gain_ref,
     key_v,
     val_v,
     gate_v,
     up_v,
     down_v,
+    gate_t,
+    up_t,
     rows_q,
     rows_res,
     hst,
@@ -68,6 +82,7 @@
     y_in,
     ret,
     r_in,
+    sem_in,
     sem_kv,
     sem_w,
     send_i,
@@ -99,61 +114,89 @@
 
     pair = (y * 2 + 1 - core, e)
 
+    smalls = []
+    for n, (src, dst) in enumerate(
+        ((q_hbm, q_ref), (res_hbm, res_ref), (ids_hbm, ids_s), (wts_hbm, wts_s), (gain_hbm, gain_ref))
+    ):
+        cp = pltpu.make_async_copy(src, dst, sem_in.at[n])
+        cp.start()
+        smalls.append(cp)
     loads = []
     for r in range(2):
         for n, (src, dst) in enumerate(((key_hbm, key_v), (val_hbm, val_v))):
             cp = pltpu.make_async_copy(src.at[r], dst.at[r], sem_kv.at[2 * r + n])
             cp.start()
             loads.append(cp)
-    w_loads = []
-    for n, (src, dst) in enumerate(((gate_hbm, gate_v), (up_hbm, up_v), (down_hbm, down_v))):
-        cp = pltpu.make_async_copy(src.at[0], dst, sem_w.at[n])
-        cp.start()
-        w_loads.append(cp)
 
     barrier = pltpu.get_barrier_semaphore()
     greet = [plane_dev(i, j) for i, j in offsets[1:]] + [y_dev(d) for d in range(1, NY)] + [pair]
     for dev in greet:
         pl.semaphore_signal(barrier, inc=1, device_id=dev, device_id_type=MESH)
 
-    sub = lax.broadcasted_iota(jnp.int32, (8, 128), 0)
-    lane = lax.broadcasted_iota(jnp.int32, (8, 128), 1)
-    tile = jnp.zeros((8, 128), F32)
+    smalls[0].wait()
+    qf = q_ref[...].astype(F32)
+    for h in range(H):
+        rows_q[pl.ds(h, 2, stride=H), :] = qf[:, h * HD : (h + 1) * HD]
+    head = lax.broadcasted_iota(jnp.int32, (H, HD), 0)
+    masks = [(head >= PER * g) & (head < PER * (g + 1)) for g in range(KVH)]
+    q_wide = []
+    for r in range(2):
+        q = rows_q[pl.ds(r * H, H), :]
+        q_wide.append(
+            jnp.concatenate([jnp.where(m, q, 0.0) for m in masks], axis=1).astype(BF)
+        )
+    smalls[1].wait()
+    rf = res_ref[...].astype(F32)
+    for h in range(H):
+        rows_res[pl.ds(h, 2, stride=H), :] = rf[:, h * HD : (h + 1) * HD]
+    for cp in smalls[2:]:
+        cp.wait()
+
+    lane = lax.broadcasted_iota(jnp.int32, (1, 128), 1)
+    tile = jnp.zeros((1, 128), F32)
     for r in range(2):
         for k in range(TOPK):
-            tile = jnp.where((sub == r) & (lane == ids_s[r, k]), 1.0, tile)
+            tile = jnp.where(lane == ids_s[r, k] + r * PLANE, 1.0, tile)
     mine_ids[...] = tile
 
-    qf = q_ref[...].astype(F32)
-    rf = res_ref[...].astype(F32)
-    for h in range(H):
-        rows_q[pl.ds(h, 2, stride=H), :] = qf[:, h * HD : (h + 1) * HD]
-        rows_res[pl.ds(h, 2, stride=H), :] = rf[:, h * HD : (h + 1) * HD]
-    head = lax.broadcasted_iota(jnp.int32, (H, HD), 0)
-    masks = [(head >= PER * g) & (head < PER * (g + 1)) for g in range(KVH)]
+    for cp in loads:
+        cp.wait()
+    w_loads = [
+        pltpu.make_async_copy(
+            src.at[0, :, pl.ds(c * CW, CW)], dst.at[:, pl.ds(c * CW, CW)], sem_w.at[2 * c + n]
+        )
+        for c in range(NC)
+        for n, (src, dst) in enumerate(((gate_hbm, gate_v), (up_hbm, up_v)))
+    ]
+    w_loads.append(pltpu.make_async_copy(down_hbm.at[0], down_v, sem_w.at[2 * NC]))
+    for cp in w_loads[: 2 * FIRST]:
+        cp.start()
+
+    def turn(c):
+        for n, (src, dst) in enumerate(((gate_v, gate_t), (up_v, up_t))):
+            w_loads[2 * c + n].wait()
+            dst[c * CW : (c + 1) * CW, :] = jnp.transpose(src[:, c * CW : (c + 1) * CW])
+
+    scores = jnp.concatenate([across(q_wide[r], key_v[r]) for r in range(2)], axis=0) * HD ** (-0.5)
+    lifted = jnp.exp(scores - jnp.max(scores, axis=1, keepdims=True))
+    probs = (lifted / jnp.sum(lifted, axis=1, keepdims=True)).astype(BF)
     gain = gain_ref[...]
+    normed = []
     for r in range(2):
-        q = rows_q[pl.ds(r * H, H), :]
-        q_wide = jnp.concatenate([jnp.where(m, q, 0.0) for m in masks], axis=1).astype(BF)
-        loads[2 * r].wait()
-        scores = lax.dot_general(
-            q_wide, key_v[r], (((1,), (1,)), ((), ())), preferred_element_type=F32
-        ) * HD ** (-0.5)
-        lifted = jnp.exp(scores - jnp.max(scores, axis=1, keepdims=True))
-        probs = (lifted / jnp.sum(lifted, axis=1, keepdims=True)).astype(BF)
-        loads[2 * r + 1].wait()
-        wide = jnp.dot(probs, val_v[r], preferred_element_type=F32)
+        wide = jnp.dot(probs[r * H : (r + 1) * H], val_v[r], preferred_element_type=F32)
         attended = jnp.zeros((H, HD), F32)
         for g in range(KVH):
             attended = jnp.where(masks[g], wide[:, g * HD : (g + 1) * HD], attended)
         hstate = (rows_res[pl.ds(r * H, H), :] + attended).astype(BF).astype(F32)
         hst[r] = hstate
-        mean = jnp.sum(hstate) * (1.0 / D)
+        mean = total_of(hstate) * (1.0 / D)
         centered = hstate - mean
-        var = jnp.sum(centered * centered) * (1.0 / D)
-        normed = (centered * lax.rsqrt(var + 1e-05) * gain).astype(BF)
-        mine[r] = normed
-        x_in[0, r] = normed
+        var = total_of(centered * centered) * (1.0 / D)
+        normed.append(centered * lax.rsqrt(var + 1e-05) * gain)
+    for c in range(NC):
+        block = jnp.concatenate([v[c * HC : (c + 1) * HC, :] for v in normed], axis=0).astype(BF)
+        mine[c] = block
+        x_in[c, 0] = block
 
     pl.semaphore_wait(barrier, len(greet))
 
@@ -167,21 +210,27 @@
         for n, (i, j) in enumerate(offsets):
             if n:
                 pltpu.make_async_remote_copy(
-                    src_ref=mine.at[:, pl.ds(c * HC, HC)],
-                    dst_ref=x_in.at[n, :, pl.ds(c * HC, HC)],
+                    src_ref=mine.at[c], dst_ref=x_in.at[c, n],
                     send_sem=send_a.at[c], recv_sem=recv_a.at[c],
                     device_id=plane_dev(i, j), device_id_type=MESH,
                 ).start()
+    for cp in w_loads[2 * FIRST :]:
+        cp.start()
+    for c in range(EARLY):
+        turn(c)
     ids_in[0] = mine_ids[...]
     bytes_wait(ids_in.at[pl.ds(1, PLANE - 1)], recv_i.at[0])
 
-    table = ids_in[...].reshape(PLANE * 8, 128)
-    rowi = lax.broadcasted_iota(jnp.int32, (2 * PLANE, PLANE * 8), 0)
-    coli = lax.broadcasted_iota(jnp.int32, (2 * PLANE, PLANE * 8), 1)
-    squeeze = jnp.where(coli == 4 * rowi - 3 * (rowi & 1), 1.0, 0.0)
-    named = jnp.dot(squeeze, table, preferred_element_type=F32)
+    table = jnp.concatenate([ids_in[n] for n in range(PLANE)], axis=0)
+    rowi = lax.broadcasted_iota(jnp.int32, (2 * PLANE, PLANE), 0)
+    coli = lax.broadcasted_iota(jnp.int32, (2 * PLANE, PLANE), 1)
+    twice = jnp.where(2 * coli == rowi - (rowi & 1), 1.0, 0.0)
+    named = jnp.dot(twice, table, preferred_element_type=F32)
+    mine_row = lax.broadcasted_iota(jnp.int32, (2 * PLANE, 128), 0)
     mine_lane = lax.broadcasted_iota(jnp.int32, (2 * PLANE, 128), 1)
-    picked_c = jnp.sum(jnp.where(mine_lane == e, named, 0.0), axis=1, keepdims=True)
+    picked_c = jnp.sum(
+        jnp.where(mine_lane == e + PLANE * (mine_row & 1), named, 0.0), axis=1, keepdims=True
+    )
     picked_b = jnp.broadcast_to(picked_c, (2 * PLANE, 128))
     ri = lax.broadcasted_iota(jnp.int32, (2 * PLANE, 2 * PLANE), 0)
     ci = lax.broadcasted_iota(jnp.int32, (2 * PLANE, 2 * PLANE), 1)
@@ -206,10 +255,8 @@
 
     pair_copies = []
     for c in range(NC):
-        bytes_wait(x_in.at[pl.ds(1, PLANE - 1), :, pl.ds(c * HC, HC)], recv_a.at[c])
-        flat[...] = (
-            x_in[:, :, c * HC : (c + 1) * HC, :].astype(F32).reshape(2 * PLANE * HC, HD)
-        )
+        bytes_wait(x_in.at[c, pl.ds(1, PLANE - 1)], recv_a.at[c])
+        flat[...] = x_in[c].astype(F32).reshape(2 * PLANE * HC, HD)
         for s in range(HC):
             x_t[:, s * HD : (s + 1) * HD] = flat[pl.ds(s, 2 * PLANE, stride=HC), :].astype(BF)
         x_all[c, 0] = jnp.dot(pick, x_t[...], preferred_element_type=F32).astype(BF)
@@ -219,28 +266,35 @@
                 recv_sem=recv_y.at[c, dy], device_id=y_dev(dy), device_id_type=MESH,
             ).start()
         pair_copies.append(forward(c, 0))
-
-    for c in range(NC):
+        if c % 2 == 1 and EARLY + c // 2 < NC:
+            turn(EARLY + c // 2)
+
+    def forward_all(c):
         for dy in range(1, NY):
             bytes_wait(x_all.at[c, dy], recv_y.at[c, dy])
             pair_copies.append(forward(c, dy))
+
+    def multiply(c):
         for dy in range(NY):
             bytes_wait(x_all.at[c, NY + dy], recv_p.at[c, dy])
-        if c == 0:
-            w_loads[0].wait()
-            w_loads[1].wait()
         block = x_all[c].reshape(2 * NY * CAP, CW)
-        gate = across(gate_v[:, c * CW : (c + 1) * CW], block)
-        up = across(up_v[:, c * CW : (c + 1) * CW], block)
+        gate = jnp.dot(block, gate_t[c * CW : (c + 1) * CW, :], preferred_element_type=F32)
+        up = jnp.dot(block, up_t[c * CW : (c + 1) * CW, :], preferred_element_type=F32)
         if c < NC - 1:
             acc_g[...] = gate if c == 0 else acc_g[...] + gate
             acc_u[...] = up if c == 0 else acc_u[...] + up
         else:
             gate = acc_g[...] + gate
             up = acc_u[...] + up
-            act[...] = jnp.transpose(gate / (1.0 + jnp.exp(-gate)) * up).astype(BF)
-
-    w_loads[2].wait()
+            act[...] = (gate / (1.0 + jnp.exp(-gate)) * up).astype(BF)
+
+    forward_all(0)
+    for c in range(NC):
+        if c < NC - 1:
+            forward_all(c + 1)
+        multiply(c)
+
+    w_loads[2 * NC].wait()
 
     def down(n):
         out = jnp.dot(
@@ -263,9 +317,10 @@
 
     for n in range(NC):
         down(n)
-        if n:
-            pair_sum(n - 1)
-    pair_sum(NC - 1)
+        if n >= LAG:
+            pair_sum(n - LAG)
+    for n in range(NC - LAG, NC):
+        pair_sum(n)
 
     for n in range(NC):
         bytes_wait(y_in.at[n], recv_z.at[n])
@@ -275,7 +330,7 @@
         back = jnp.dot(spread, total.astype(BF), preferred_element_type=F32)
         for s in range(HC):
             flat[pl.ds(s, 2 * PLANE, stride=HC), :] = back[:, s * HD : (s + 1) * HD]
-        ret[n] = flat[...].astype(BF).reshape(PLANE, 2, HC, HD)
+        ret[n] = flat[...].astype(BF).reshape(PLANE, 2 * HC, HD)
         for m, (i, j) in enumerate(offsets):
             if m:
                 pltpu.make_async_remote_copy(
@@ -295,16 +350,19 @@
         weights.append(row)
     for n in range(NC):
         bytes_wait(r_in.at[n, pl.ds(1, PLANE - 1)], recv_r.at[n])
+        replies = [ret[n, 0].astype(F32)] + [r_in[n, m].astype(F32) for m in range(1, PLANE)]
         for r in range(2):
             total = hst[r, n * HC : (n + 1) * HC, :]
             for m in range(PLANE):
-                got = ret[n, 0, r] if m == 0 else r_in[n, m, r]
-                total = total + weights[r][m] * got.astype(F32)
-            out_ref[r, n * HC : (n + 1) * HC, :] = total.astype(BF)
+                got = replies[m][r * HC : (r + 1) * HC, :]
+                total = total + weights[r][m] * got
+            rows_q[pl.ds(r * H + n * HC, HC), :] = total
+    for h in range(H):
+        out_ref[:, h * HD : (h + 1) * HD] = rows_q[pl.ds(h, 2, stride=H), :].astype(BF)
 
     bytes_wait(ids_in.at[pl.ds(1, PLANE - 1)], send_i.at[0])
     for c in range(NC):
-        bytes_wait(x_in.at[pl.ds(1, PLANE - 1), :, pl.ds(c * HC, HC)], send_a.at[c])
+        bytes_wait(x_in.at[c, pl.ds(1, PLANE - 1)], send_a.at[c])
         bytes_wait(x_all.at[c, pl.ds(1, NY - 1)], send_y.at[c])
         bytes_wait(pair_in.at[c], send_q.at[c])
         bytes_wait(y_in.at[c], send_z.at[c])
@@ -315,41 +373,48 @@
 
 def body(q, key_cache, value_cache, residual, norm_gain, ids, wts, w_gate, w_up, w_down):
     vmem = pl.BlockSpec(memory_space=pltpu.VMEM)
-    smem = pl.BlockSpec(memory_space=pltpu.SMEM)
     hbm = pl.BlockSpec(memory_space=pl.ANY)
     dma = pltpu.SemaphoreType.DMA
     out = pl.pallas_call(
         kernel,
-        out_shape=jax.ShapeDtypeStruct((2, H, HD), BF),
-        in_specs=[smem, smem, vmem, vmem, vmem] + [hbm] * 5,
+        out_shape=jax.ShapeDtypeStruct((2, D), BF),
+        in_specs=[hbm] * 10,
         out_specs=vmem,
         scratch_shapes=[
+            pltpu.SMEM((2, TOPK), jnp.int32),
+            pltpu.SMEM((2, TOPK), F32),
+            pltpu.VMEM((2, D), BF),
+            pltpu.VMEM((2, D), BF),
+            pltpu.VMEM((H, HD), F32),
             pltpu.VMEM((2, CTX, KVH * HD), BF),
             pltpu.VMEM((2, CTX, KVH * HD), BF),
             pltpu.VMEM((FF, D), BF),
             pltpu.VMEM((FF, D), BF),
             pltpu.VMEM((FF, D), BF),
+            pltpu.VMEM((D, FF), BF),
+            pltpu.VMEM((D, FF), BF),
             pltpu.VMEM((2 * H, HD), F32),
             pltpu.VMEM((2 * H, HD), F32),
             pltpu.VMEM((2, H, HD), F32),
-            pltpu.VMEM((2, H, HD), BF),
-            pltpu.VMEM((8, 128), F32),
-            pltpu.VMEM((PLANE, 8, 128), F32),
-            pltpu.VMEM((PLANE, 2, H, HD), BF),
+            pltpu.VMEM((NC, 2 * HC, HD), BF),
+            pltpu.VMEM((1, 128), F32),
+            pltpu.VMEM((PLANE, 1, 128), F32),
+            pltpu.VMEM((NC, PLANE, 2 * HC, HD), BF),
             pltpu.VMEM((2 * PLANE * HC, HD), F32),
             pltpu.VMEM((2 * PLANE, CW), BF),
             pltpu.VMEM((NC, 2 * NY, CAP, CW), BF),
-            pltpu.VMEM((FF, 2 * NY * CAP), F32),
-            pltpu.VMEM((FF, 2 * NY * CAP), F32),
+            pltpu.VMEM((2 * NY * CAP, FF), F32),
+            pltpu.VMEM((2 * NY * CAP, FF), F32),
             pltpu.VMEM((2 * NY * CAP, FF), BF),
             pltpu.VMEM((NC, 2 * NY, CAP, CW), BF),
             pltpu.VMEM((NC, NY, CAP, CW), BF),
             pltpu.VMEM((NC, NY, CAP, CW), BF),
             pltpu.VMEM((NC, NY - 1, CAP, CW), BF),
-            pltpu.VMEM((NC, PLANE, 2, HC, HD), BF),
-            pltpu.VMEM((NC, PLANE, 2, HC, HD), BF),
+            pltpu.VMEM((NC, PLANE, 2 * HC, HD), BF),
+            pltpu.VMEM((NC, PLANE, 2 * HC, HD), BF),
+            dma((5,)),
             dma((4,)),
-            dma((3,)),
+            dma((2 * NC + 1,)),
             dma((1,)),
             dma((1,)),
             dma((NC,)),
@@ -366,7 +431,7 @@
             dma((NC,)),
         ],
         compiler_params=pltpu.CompilerParams(
-            collective_id=0, has_side_effects=True, vmem_limit_bytes=56 * 1024 * 1024
+            collective_id=0, has_side_effects=True, vmem_limit_bytes=62 * 1024 * 1024
         ),
         cost_estimate=pl.CostEstimate(
             flops=6 * 128 * D * FF, bytes_accessed=3 * 2 * D * FF, transcendentals=128 * FF
@@ -384,7 +449,7 @@
         jnp.swapaxes(w_up, 1, 2),
         w_down,
     )
-    return out.reshape(2, D)
+    return out
 
 
 def solution(mesh):

time: 51.9 us -> 45.5 us (0.88)
  Pallas kernels: 50.3 us -> 43.9 us
    pallas_call x1, Pallas kernels: 50.3 us -> 43.9 us  [body(): pl.pallas_call(kernel, out_shape=jax.ShapeDtypeStruct((2, D), BF), in_spe...]
where the time goes in v2:
time: 45.5 us; the launch traced here: 45.3 us
  Pallas kernels  43.9 us (96%)
  local copies, waits for them, and re-layouts  1.36 us (3%)
    pallas_call x1, Pallas kernels, body(): pl.pallas_call(kernel, out_shape=jax.ShapeDtypeStruct((2, D), BF), in_spe...  43.9 us
    unnamed x1, local copies, waits for them, and re-layouts  1.36 us

profile of v2, /device:TPU:0, one launch (start us, length us, event | category | flops | bytes accessed | tf_op | source)
XLA Modules:
  0.0 45.3 jit_solution(9123110369247509791)
XLA Ops:
  0.0 43.9 %decode_layer.1 = bf16[2,6144]{1,0:T(2,128)(2,1)} custom-call(s32[2,4]{1,0:T(2,128)} %ids_hbm.1, f32[2,4]{1,0:T(2,128)} %wts_hbm.1, bf16[2,6144]{1,0:T(2,128)(2,1)} %q_hbm.1, bf16[2,6144]{1,0:T(2,128)(2,1)} %res_hbm.1, f32[48,128]{1,0:T(8,128)} %bitcast.5, bf16[2,128,1024]{2,1,0:T(8,128)(2,1)} %key_hbm.1, bf16[2,128,1024]{2,1,0:T(8,128)(2,1)} %val_hbm.1, ...), custom_call_target="tpu_custom_call" | custom-call | flops 3170893824 | bytes 24772608 | tf_op jit(solution)/shard_map/decode_layer/pallas_call | solution.py:378
  43.9 1.4 %copy.12 = bf16[2,6144]{1,0:T(2,128)(2,1)} copy(bf16[2,6144]{1,0:T(2,128)(2,1)} %decode_layer.1) | data formatting | bytes 49152

commit v3 on v2

--- a/solution.py
+++ b/solution.py
@@ -19,6 +19,7 @@
 FF = 672
 NC = 6
 LAG = 3
+DELAY = 6
 EARLY = 4
 FIRST = 4
 HC = H // NC
@@ -80,6 +81,7 @@
     pair_in,
     summed,
     y_in,
+    joint,
     ret,
     r_in,
     sem_in,
@@ -95,6 +97,10 @@
     recv_p,
     send_q,
     recv_q,
+    send_f,
+    recv_f,
+    send_j,
+    recv_j,
     send_z,
     recv_z,
     send_r,
@@ -113,6 +119,7 @@
         return (lax.rem(y + dy + NY, NY) * 2 + core, e)
 
     pair = (y * 2 + 1 - core, e)
+    side = 1 - 2 * core
 
     smalls = []
     for n, (src, dst) in enumerate(
@@ -309,24 +316,44 @@
     def pair_sum(n):
         bytes_wait(pair_in.at[n], recv_q.at[n])
         summed[n] = (part[n, :NY].astype(F32) + pair_in[n].astype(F32)).astype(BF)
-        for dy in range(1, NY):
-            pltpu.make_async_remote_copy(
-                src_ref=summed.at[n, dy], dst_ref=y_in.at[n, dy - 1], send_sem=send_z.at[n],
-                recv_sem=recv_z.at[n], device_id=y_dev(-dy), device_id_type=MESH,
-            ).start()
+        pltpu.make_async_remote_copy(
+            src_ref=summed.at[n, 2], dst_ref=y_in.at[n, 2], send_sem=send_f.at[n],
+            recv_sem=recv_f.at[n], device_id=y_dev(side), device_id_type=MESH,
+        ).start()
+
+    def direct(n):
+        pltpu.make_async_remote_copy(
+            src_ref=summed.at[n, 1 + 2 * core], dst_ref=y_in.at[n, 0], send_sem=send_z.at[n],
+            recv_sem=recv_z.at[n], device_id=y_dev(-side), device_id_type=MESH,
+        ).start()
+
+    def combine(n):
+        bytes_wait(y_in.at[n, 2], recv_f.at[n])
+        joint[n] = (summed[n, 3 - 2 * core].astype(F32) + y_in[n, 2].astype(F32)).astype(BF)
+        pltpu.make_async_remote_copy(
+            src_ref=joint.at[n], dst_ref=y_in.at[n, 1], send_sem=send_j.at[n],
+            recv_sem=recv_j.at[n], device_id=y_dev(side), device_id_type=MESH,
+        ).start()
 
     for n in range(NC):
         down(n)
         if n >= LAG:
             pair_sum(n - LAG)
+            if n - LAG >= DELAY:
+                direct(n - LAG - DELAY)
     for n in range(NC - LAG, NC):
         pair_sum(n)
-
+        if n >= DELAY:
+            direct(n - DELAY)
+    for n in range(NC - DELAY, NC):
+        direct(n)
     for n in range(NC):
-        bytes_wait(y_in.at[n], recv_z.at[n])
-        total = summed[n, 0].astype(F32)
-        for dy in range(NY - 1):
-            total = total + y_in[n, dy].astype(F32)
+        combine(n)
+
+    for n in range(NC):
+        bytes_wait(y_in.at[n, 0], recv_z.at[n])
+        bytes_wait(y_in.at[n, 1], recv_j.at[n])
+        total = summed[n, 0].astype(F32) + y_in[n, 0].astype(F32) + y_in[n, 1].astype(F32)
         back = jnp.dot(spread, total.astype(BF), preferred_element_type=F32)
         for s in range(HC):
             flat[pl.ds(s, 2 * PLANE, stride=HC), :] = back[:, s * HD : (s + 1) * HD]
@@ -365,7 +392,9 @@
         bytes_wait(x_in.at[c, pl.ds(1, PLANE - 1)], send_a.at[c])
         bytes_wait(x_all.at[c, pl.ds(1, NY - 1)], send_y.at[c])
         bytes_wait(pair_in.at[c], send_q.at[c])
-        bytes_wait(y_in.at[c], send_z.at[c])
+        bytes_wait(y_in.at[c, 0], send_z.at[c])
+        bytes_wait(y_in.at[c, 2], send_f.at[c])
+        bytes_wait(joint.at[c], send_j.at[c])
         bytes_wait(r_in.at[c, pl.ds(1, PLANE - 1)], send_r.at[c])
     for cp in pair_copies:
         cp.wait_send()
@@ -410,6 +439,7 @@
             pltpu.VMEM((NC, NY, CAP, CW), BF),
             pltpu.VMEM((NC, NY, CAP, CW), BF),
             pltpu.VMEM((NC, NY - 1, CAP, CW), BF),
+            pltpu.VMEM((NC, CAP, CW), BF),
             pltpu.VMEM((NC, PLANE, 2 * HC, HD), BF),
             pltpu.VMEM((NC, PLANE, 2 * HC, HD), BF),
             dma((5,)),
@@ -423,6 +453,10 @@
             dma((NC, NY)),
             dma((NC, NY)),
             dma((NC, NY)),
+            dma((NC,)),
+            dma((NC,)),
+            dma((NC,)),
+            dma((NC,)),
             dma((NC,)),
             dma((NC,)),
             dma((NC,)),

time: 45.5 us -> 44.1 us (0.969)
  Pallas kernels: 43.9 us -> 42.6 us
    pallas_call x1, Pallas kernels: 43.9 us -> 42.6 us  [body(): pl.pallas_call(kernel, out_shape=jax.ShapeDtypeStruct((2, D), BF), in_spe...]
where the time goes in v3:
time: 44.1 us; the launch traced here: 44 us
  Pallas kernels  42.6 us (97%)
  local copies, waits for them, and re-layouts  1.36 us (3%)
    pallas_call x1, Pallas kernels, body(): pl.pallas_call(kernel, out_shape=jax.ShapeDtypeStruct((2, D), BF), in_spe...  42.6 us
    unnamed x1, local copies, waits for them, and re-layouts  1.36 us

profile of v3, /device:TPU:0, one launch (start us, length us, event | category | flops | bytes accessed | tf_op | source)
XLA Modules:
  0.0 44.0 jit_solution(15300702954837132650)
XLA Ops:
  0.0 42.6 %decode_layer.1 = bf16[2,6144]{1,0:T(2,128)(2,1)} custom-call(s32[2,4]{1,0:T(2,128)} %ids_hbm.1, f32[2,4]{1,0:T(2,128)} %wts_hbm.1, bf16[2,6144]{1,0:T(2,128)(2,1)} %q_hbm.1, bf16[2,6144]{1,0:T(2,128)(2,1)} %res_hbm.1, f32[48,128]{1,0:T(8,128)} %bitcast.5, bf16[2,128,1024]{2,1,0:T(8,128)(2,1)} %key_hbm.1, bf16[2,128,1024]{2,1,0:T(8,128)(2,1)} %val_hbm.1, ...), custom_call_target="tpu_custom_call" | custom-call | flops 3170893824 | bytes 24772608 | tf_op jit(solution)/shard_map/decode_layer/pallas_call | solution.py:407
  42.6 1.4 %copy.12 = bf16[2,6144]{1,0:T(2,128)(2,1)} copy(bf16[2,6144]{1,0:T(2,128)(2,1)} %decode_layer.1) | data formatting | bytes 49152

commit v4 on v3

--- a/solution.py
+++ b/solution.py
@@ -129,11 +129,11 @@
         cp.start()
         smalls.append(cp)
     loads = []
-    for r in range(2):
-        for n, (src, dst) in enumerate(((key_hbm, key_v), (val_hbm, val_v))):
-            cp = pltpu.make_async_copy(src.at[r], dst.at[r], sem_kv.at[2 * r + n])
-            cp.start()
-            loads.append(cp)
+    for r, n in ((0, 0), (1, 0), (0, 1), (1, 1)):
+        src, dst = ((key_hbm, key_v), (val_hbm, val_v))[n]
+        cp = pltpu.make_async_copy(src.at[r], dst.at[r], sem_kv.at[2 * r + n])
+        cp.start()
+        loads.append(cp)
 
     barrier = pltpu.get_barrier_semaphore()
     greet = [plane_dev(i, j) for i, j in offsets[1:]] + [y_dev(d) for d in range(1, NY)] + [pair]
@@ -166,7 +166,10 @@
             tile = jnp.where(lane == ids_s[r, k] + r * PLANE, 1.0, tile)
     mine_ids[...] = tile
 
-    for cp in loads:
+    for cp in loads[:2]:
+        cp.wait()
+    scores = jnp.concatenate([across(q_wide[r], key_v[r]) for r in range(2)], axis=0) * HD ** (-0.5)
+    for cp in loads[2:]:
         cp.wait()
     w_loads = [
         pltpu.make_async_copy(
@@ -184,7 +187,6 @@
             w_loads[2 * c + n].wait()
             dst[c * CW : (c + 1) * CW, :] = jnp.transpose(src[:, c * CW : (c + 1) * CW])
 
-    scores = jnp.concatenate([across(q_wide[r], key_v[r]) for r in range(2)], axis=0) * HD ** (-0.5)
     lifted = jnp.exp(scores - jnp.max(scores, axis=1, keepdims=True))
     probs = (lifted / jnp.sum(lifted, axis=1, keepdims=True)).astype(BF)
     gain = gain_ref[...]
@@ -252,10 +254,12 @@
         spread_f, ident, (((0,), (0,)), ((), ())), preferred_element_type=F32
     )[:CAP, :].astype(BF)
 
-    def forward(c, dy):
+    def forward(c, first, count):
         cp = pltpu.make_async_remote_copy(
-            src_ref=x_all.at[c, dy], dst_ref=x_all.at[c, NY + dy], send_sem=send_p.at[c, dy],
-            recv_sem=recv_p.at[c, dy], device_id=pair, device_id_type=MESH,
+            src_ref=x_all.at[c, pl.ds(first, count)],
+            dst_ref=x_all.at[c, pl.ds(NY + first, count)],
+            send_sem=send_p.at[c, min(first, 1)], recv_sem=recv_p.at[c],
+            device_id=pair, device_id_type=MESH,
         )
         cp.start()
         return cp
@@ -270,20 +274,18 @@
         for dy in range(1, NY):
             pltpu.make_async_remote_copy(
                 src_ref=x_all.at[c, 0], dst_ref=x_all.at[c, dy], send_sem=send_y.at[c],
-                recv_sem=recv_y.at[c, dy], device_id=y_dev(dy), device_id_type=MESH,
+                recv_sem=recv_y.at[c], device_id=y_dev(dy), device_id_type=MESH,
             ).start()
-        pair_copies.append(forward(c, 0))
+        pair_copies.append(forward(c, 0, 1))
         if c % 2 == 1 and EARLY + c // 2 < NC:
             turn(EARLY + c // 2)
 
     def forward_all(c):
-        for dy in range(1, NY):
-            bytes_wait(x_all.at[c, dy], recv_y.at[c, dy])
-            pair_copies.append(forward(c, dy))
+        bytes_wait(x_all.at[c, pl.ds(1, NY - 1)], recv_y.at[c])
+        pair_copies.append(forward(c, 1, NY - 1))
 
     def multiply(c):
-        for dy in range(NY):
-            bytes_wait(x_all.at[c, NY + dy], recv_p.at[c, dy])
+        bytes_wait(x_all.at[c, pl.ds(NY, NY)], recv_p.at[c])
         block = x_all[c].reshape(2 * NY * CAP, CW)
         gate = jnp.dot(block, gate_t[c * CW : (c + 1) * CW, :], preferred_element_type=F32)
         up = jnp.dot(block, up_t[c * CW : (c + 1) * CW, :], preferred_element_type=F32)
@@ -450,9 +452,9 @@
             dma((NC,)),
             dma((NC,)),
             dma((NC,)),
-            dma((NC, NY)),
-            dma((NC, NY)),
-            dma((NC, NY)),
+            dma((NC,)),
+            dma((NC, 2)),
+            dma((NC,)),
             dma((NC,)),
             dma((NC,)),
             dma((NC,)),

time: 44.1 us -> 43.7 us (level)
  no operation moved by 1% of the time
where the time goes in v4:
time: 43.7 us; the launch traced here: 43.6 us
  Pallas kernels  42.2 us (97%)
  local copies, waits for them, and re-layouts  1.36 us (3%)
    pallas_call x1, Pallas kernels, body(): pl.pallas_call(kernel, out_shape=jax.ShapeDtypeStruct((2, D), BF), in_spe...  42.2 us
    unnamed x1, local copies, waits for them, and re-layouts  1.36 us

profile of v4, /device:TPU:0, one launch (start us, length us, event | category | flops | bytes accessed | tf_op | source)
XLA Modules:
  0.0 43.6 jit_solution(13900384509822875557)
XLA Ops:
  0.0 42.2 %decode_layer.1 = bf16[2,6144]{1,0:T(2,128)(2,1)} custom-call(s32[2,4]{1,0:T(2,128)} %ids_hbm.1, f32[2,4]{1,0:T(2,128)} %wts_hbm.1, bf16[2,6144]{1,0:T(2,128)(2,1)} %q_hbm.1, bf16[2,6144]{1,0:T(2,128)(2,1)} %res_hbm.1, f32[48,128]{1,0:T(8,128)} %bitcast.5, bf16[2,128,1024]{2,1,0:T(8,128)(2,1)} %key_hbm.1, bf16[2,128,1024]{2,1,0:T(8,128)(2,1)} %val_hbm.1, ...), custom_call_target="tpu_custom_call" | custom-call | flops 3170893824 | bytes 24772608 | tf_op jit(solution)/shard_map/decode_layer/pallas_call | solution.py:409
  42.2 1.4 %copy.12 = bf16[2,6144]{1,0:T(2,128)(2,1)} copy(bf16[2,6144]{1,0:T(2,128)(2,1)} %decode_layer.1) | data formatting | bytes 49152
